TPU v7x, 32 devices: a whole 2x2x4 slice. The times are simulated.
32 devices in a mesh: seq: 1, res: 32 (over z, y, x, core).
Axes of the slice: x: 2, y: 2, z: 4, core: 2. Of those that a mesh axis runs over, the one named last changes fastest.
Arguments:
- extra_activations: bfloat16 [32, 65536], P('seq', 'res'), may hold values from -6 to 6
- twofold_representation: bfloat16 [1024, 1024, 128], P('res', 'seq'), may hold values from -6 to 6
- present_indicator: int32 [32, 1024], P('seq', 'res'), may hold values 0 or 1
- amino_presence: int32 [1024], P('res'), may hold values 0 or 1
- twofold_offset_matrix: bfloat16 [128, 8], replicated, may hold values from -1.5859375 to 1.5859375
- horizontal_matrix: bfloat16 [64, 256], replicated, may hold values from -8 to 8, as said below
- horizontal_exit_matrix: bfloat16 [64, 64], replicated, may hold values from -1.5 to 1.5
- vertical_matrix: bfloat16 [64, 144], replicated, may hold values from -8 to 8, as said below
- vertical_exit_matrix: bfloat16 [64, 64], replicated, may hold values from -0.75 to 0.75
Outputs:
- msa_out: bfloat16 [32, 65536], P('seq', 'res')
Inputs may be any that keep to these rules, and one draw needn't show every extreme that they name: `horizontal_matrix`: a projection matrix. `vertical_matrix`: a projection matrix.
All inputs are finite; a program needn't handle non-finite values. No bound on the sum of `present_indicator` or of `amino_presence` on one device may be relied on, other than what follows from the above.
Results may differ from a plain program's by a relative error of at most 0.02.
The roundings to bfloat16 on the way count: a program that leaves them out, or rounds other values in their place, can miss the bound.
Values may be sent and summed in bfloat16 or wider, within the bound.
No kernel may reach another device: no remote copies, remote signals or barrier semaphores. Data moves between devices by JAX's collectives and lax.ppermute only.
A program may use at most 64 MiB of HBM per device.

v0:
```python
import functools
import math

import jax
import jax.numpy as jnp
from jax import lax
from jax.experimental import pallas as pl
from jax.experimental.pallas import tpu as pltpu
from jax.sharding import PartitionSpec as P

F32 = jnp.float32
BF16 = jnp.bfloat16
LOG2E = math.log2(math.e)
EPS = 1e-05

NT = (((1,), (1,)), ((), ()))


def mm(a, b):
    return jnp.dot(a, b, preferred_element_type=F32)


def mm_nt(a, b):
    return lax.dot_general(a, b, NT, preferred_element_type=F32)


def iota(shape, axis):
    return lax.broadcasted_iota(jnp.int32, shape, axis)


def one_hot(condition):
    return jnp.where(condition, 1.0, 0.0).astype(BF16)


def block_matrix(size, block, on_diagonal, elsewhere):
    row, col = iota((size, 1), 0), iota((1, size), 1)
    inside = jnp.where(row == col, on_diagonal, elsewhere)
    return jnp.where(row // block == col // block, inside, 0.0).astype(BF16)


def halves(value):
    high = value.astype(BF16)
    return high, (value - high.astype(F32)).astype(BF16)


def mm_split(value, matrix):
    high, low = halves(value)
    return mm(high, matrix) + mm(low, matrix)


def paired_norm(x, width):
    lanes = x.shape[1]
    centre = mm(x, block_matrix(lanes, width, 1.0 - 1.0 / width, -1.0 / width))
    spread = mm_split(centre * centre, block_matrix(lanes, width, 1.0 / width, 1.0 / width))
    return (centre * lax.rsqrt(spread + EPS)).astype(BF16)


def row_shuffle(rows, inner, outer):
    total = rows.shape[0]
    row, col = iota((total, 1), 0), iota((1, total), 1)
    return mm(one_hot(col == (row % inner) * outer + row // inner), rows).astype(BF16)


def prep_kernel(groups, me_ref, m_ref, kept_ref, *refs):
    keep_ref, send_ref, line_ref, normed_ref, spread_ref = refs
    lines, width = m_ref.shape
    pairs = width // 128
    stacked = jnp.concatenate([m_ref[:, t * 128 : (t + 1) * 128] for t in range(pairs)], axis=0)
    normed = paired_norm(stacked, 64)
    both = row_shuffle(jnp.concatenate([normed, stacked], axis=1), pairs, lines)
    normed_ref[...] = both[:, :128]
    line_ref[...] = both[:, 128:]
    kept = kept_ref[...]
    size = lines // (2 * groups)
    residues = 2 * pairs
    row, col = iota((pairs, residues), 0), iota((pairs, residues), 1)
    evens, odds = one_hot(col == 2 * row), one_hot(col == 2 * row + 1)
    row, col = iota((128, lines), 0) - 64, iota((128, lines), 1)
    core = me_ref[0] % 2
    for n in range(2 * groups):
        start = jnp.where(n // groups == core, 0, 2 * size)
        chosen = (row >= start) & (row < start + 2 * size) & (row % size == col - n * size)
        spread = mm(one_hot(chosen), kept).astype(BF16)
        first = iota((pairs, 128), 1) < 64 + size + start
        spread_ref[n] = jnp.where(first, mm_nt(evens, spread), mm_nt(odds, spread)).astype(BF16)
    rows = size * pairs
    for ref, half in ((keep_ref, core), (send_ref, 1 - core)):
        for g in range(groups):
            index = half * groups + g
            ref[g, :rows] = normed_ref[pl.ds(pl.multiple_of(index * rows, rows), rows), :]
            ref[g, rows:] = spread_ref[index]


def bias_kernel(whole, pieces, x_ref, w_ref, after_ref, me_ref, *refs):
    outs, (acc_ref, centring_ref, wide_ref) = refs[:-3], refs[-3:]
    step = pl.program_id(0)
    heads = w_ref.shape[0]
    per_step, keys, channels = x_ref.shape
    residues = per_step * pl.num_programs(0)
    pairs = residues // 2
    tiles = acc_ref.shape[0]
    width = tiles * 128

    @pl.when(step == 0)
    def _():
        centring_ref[...] = block_matrix(
            2 * channels, channels, 1.0 - 1.0 / channels, -1.0 / channels
        )
        spread = one_hot(iota((heads, 1), 0) == iota((1, width), 1) // residues)
        wide_ref[...] = lax.dot_general(
            w_ref[...], spread, (((0,), (0,)), ((), ())), preferred_element_type=F32
        )
        acc_ref[...] = jnp.zeros(acc_ref.shape, F32)

    lane = iota((1, width), 1) % residues
    placed = []
    for n in range(per_step):
        residue = step * per_step + n
        mine = lane == (residue % 2) * pairs + residue // 2
        placed.append(jnp.where(mine, wide_ref[...], 0.0).astype(BF16))
    placed = jnp.concatenate(placed, axis=0)
    centring = centring_ref[...]
    piece = min(512, keys)
    for r in range(0, keys, piece):
        normed = []
        for n in range(0, per_step, 2):
            x = jnp.concatenate([x_ref[n, r : r + piece], x_ref[n + 1, r : r + piece]], axis=1)
            centre = mm(x, centring)
            for part in (centre[:, :channels], centre[:, channels:]):
                spread = jnp.mean(part * part, axis=-1, keepdims=True)
                normed.append((part * lax.rsqrt(spread + EPS)).astype(BF16))
        added = mm(jnp.concatenate(normed, axis=1), placed)
        for n in range(tiles):
            acc_ref[n, r : r + piece, :] += added[:, n * 128 : (n + 1) * 128]

    @pl.when(step == pl.num_programs(0) - 1)
    def _():
        if not whole:
            for n in range(tiles):
                outs[0][n * 128 : (n + 1) * 128, :] = acc_ref[n].T.astype(BF16)
            return
        levels = keys // (2 * pieces * residues)
        for flip in range(2):
            user = me_ref[0] ^ flip
            starts = [
                (user ^ (c + 2 * q + 2 * pieces * k)) * residues + p
                for q in range(pieces)
                for p in range(2)
                for k in range(levels)
                for c in range(2)
            ]
            for n in range(tiles):
                for at in range(0, keys, 128):
                    rows = [
                        acc_ref[n, pl.ds(start, pairs, stride=2), :]
                        for start in starts[at // pairs : (at + 128) // pairs]
                    ]
                    turned = jnp.concatenate(rows, axis=0).T.astype(BF16)
                    outs[flip][n * 128 : (n + 1) * 128, at : at + 128] = turned


def order_kernel(residues, pieces, me_ref, bias_ref, own_ref, send_ref):
    rows, keys = bias_ref.shape
    pairs = residues // 2
    lane = iota((1, keys), 1)
    each = keys // pieces
    which, rest = lane // each, lane % each
    parity, rest = rest // (each // 2), rest % (each // 2)
    place, pair = rest // pairs, rest % pairs
    for flip, out_ref in enumerate((own_ref, send_ref)):
        device = me_ref[0] ^ flip ^ ((place % 2) + 2 * which + 2 * pieces * (place // 2))
        target = device * residues + 2 * pair + parity
        total = jnp.zeros((rows, keys), F32)
        for start in range(0, keys, 256):
            chosen = one_hot(iota((256, keys), 0) + start == target)
            total = total + mm(bias_ref[:, start : start + 256], chosen)
        out_ref[...] = total.astype(BF16)


def pair_matrix(matrix, chosen):
    rows, columns = matrix.shape
    lane = iota((1, 128), 1)
    twice_rows = one_hot(iota((128, 1), 0) % rows == iota((1, rows), 1))
    picked = one_hot(iota((columns, 1), 0) == chosen)
    wide = mm(mm(twice_rows, matrix).astype(BF16), picked)
    same = iota((128, 1), 0) // rows == lane // (128 // 2)
    return jnp.where(same, wide, 0.0).astype(BF16)


def value_matrix(matrix, hidden, heads):
    depth = hidden // heads
    row, col = iota((128, 1), 0), iota((1, 256), 1)
    picked = one_hot(iota((4 * hidden, 1), 0) == 2 * hidden + col % hidden)
    picked = jnp.where(col < 128, picked, jnp.zeros_like(picked))
    wv = mm(mm(one_hot(row == iota((1, hidden), 1)), matrix).astype(BF16), picked)
    counted = (row >= hidden) & (col >= 128)
    wv = jnp.where(counted, 1.0 / (128 - hidden), wv)
    owner = col % 128 // depth
    return [
        jnp.where(owner == p * heads + h, wv, 0.0).astype(BF16)
        for h in range(heads)
        for p in range(2)
    ]


def query_kernel(
    groups, size, pairs, heads, own_ref, peer_ref, keep_ref, received_ref, w_ref, exit_ref,
    column_ref, column_exit_ref, kept_ref, *refs
):
    column_refs = refs[:groups]
    bias_ref, lhs_ref, sums_ref, wv_ref, gate_ref, final_ref, kept_wide_ref = refs[groups:]
    rows = own_ref.shape[0]
    bias_ref[:rows, :] = own_ref[...].astype(F32) * LOG2E
    bias_ref[rows:, :] = peer_ref[...].astype(F32) * LOG2E

    hidden = w_ref.shape[0]
    depth = hidden // heads
    lane = iota((1, 128), 1)
    wq = pair_matrix(w_ref[...], lane % hidden)
    wg = pair_matrix(w_ref[...], 3 * hidden + lane % hidden)
    for n, part in enumerate(value_matrix(w_ref[...], hidden, heads)):
        wv_ref[n * 128 : (n + 1) * 128, :] = part
    final = [
        (exit_ref, lane % hidden),
        (column_exit_ref, lane % hidden),
        (column_ref, lane % hidden),
        (column_ref, hidden + lane % hidden),
        (column_ref, 2 * hidden + lane % depth),
        (column_ref, 2 * hidden + depth + lane % depth),
    ]
    for n, (ref, chosen) in enumerate(final):
        final_ref[:, n * 128 : (n + 1) * 128] = pair_matrix(ref[...], chosen)
    total, lines = kept_wide_ref.shape[0], kept_ref.shape[0]
    spread = mm(one_hot(iota((total, 1), 0) // pairs == iota((1, lines), 1)), kept_ref[...])
    mine = iota((1, 2 * pairs), 1) // 2 == iota((total, 1), 0) % pairs
    sides = one_hot(iota((2 * pairs, 1), 0) % 2 == lane // 64)
    kept_wide_ref[...] = mm(jnp.where(mine, spread, 0.0).astype(BF16), sides)
    picked = one_hot(iota((1, 4 * hidden), 1) == hidden + iota((128, 1), 0) % hidden)
    wk = mm_nt(picked, w_ref[...]).astype(BF16)
    wk = mm(wk, one_hot(iota((hidden, 1), 0) == iota((1, 128), 1))).astype(BF16)
    lead = size * pairs
    spare = lane - hidden
    for g in range(groups):
        for n, ref in enumerate((keep_ref, received_ref)):
            gate_ref[n, g * lead : (g + 1) * lead] = jax.nn.sigmoid(mm(ref[g, :lead], wg))
            query = (mm(ref[g, :lead], wq) * (depth**-0.5)).astype(BF16).astype(F32)
            for s in range(size):
                q = query[s * pairs : (s + 1) * pairs]
                spread = [
                    jnp.where(lane // depth == p * heads + h, q, 0.0).astype(BF16)
                    for h in range(heads)
                    for p in range(2)
                ]
                folded = mm(jnp.concatenate(spread, axis=0), wk) * LOG2E
                picks = (spare >= 0) & (spare < 4 * size) & (spare % size == s)
                lhs_ref[g * size + s, n * rows : (n + 1) * rows, :] = jnp.where(
                    picks, 1.0, folded
                ).astype(BF16)
    add_pieces(groups, size, pairs, (0,) * groups, lhs_ref, bias_ref, None, column_refs, sums_ref)


def masks_of(ref, size, pairs):
    start = 2 * size * pairs
    lane = iota((1, 128), 1) - 64
    masks = []
    for p in range(2):
        blocks = []
        for k in range(ref.shape[0]):
            hidden = (1e9 * LOG2E) * (ref[k, start : start + pairs, :].astype(F32) - 1.0)
            for c in range(2):
                first = (2 * c + p) * size
                mine = (lane >= first) & (lane < first + size)
                blocks.append(jnp.where(mine, hidden, 0.0).astype(BF16))
        masks.append(jnp.concatenate(blocks, axis=0))
    return masks


def keys_of(ref, masks, s, size, pairs):
    start = s * pairs
    if not isinstance(s, int):
        start = pl.multiple_of(start, pairs)
    even = jnp.concatenate(
        [
            ref[k, pl.ds(c * size * pairs + start, pairs), :]
            for k in range(ref.shape[0])
            for c in range(2)
        ],
        axis=0,
    )
    odd = pltpu.roll(even.astype(F32), 64, 1).astype(BF16)
    low = iota(even.shape, 1) < 64
    one = jnp.ones_like(even)
    keyed = [jnp.where(low, x, m) for x, m in zip((even, odd), masks)]
    valued = [jnp.where(low, x, one) for x in (even, odd)]
    return jnp.concatenate(keyed, axis=0), jnp.concatenate(valued, axis=0)


def weigh(lhs, bias_ref, piece, keyed):
    width = keyed.shape[0]
    logits = mm_nt(lhs, keyed) + bias_ref[:, piece * width : (piece + 1) * width]
    return jnp.exp2(logits).astype(BF16)


def each_line(groups, size, pairs, places, lhs_ref, bias_ref, piece_refs, use):
    masks = [masks_of(ref, size, pairs) for ref in piece_refs]

    def weights_of(s, g):
        keyed, valued = keys_of(piece_refs[g], masks[g], s, size, pairs)
        return weigh(lhs_ref[g * size + s], bias_ref, places[g], keyed), valued

    order = [(s, g) for s in range(size) for g in range(groups)]
    ahead = weights_of(*order[0])
    for n, (s, g) in enumerate(order):
        now, ahead = ahead, weights_of(*order[n + 1]) if n + 1 < len(order) else None
        use(g * size + s, mm(*now))


def add_pieces(groups, size, pairs, places, lhs_ref, bias_ref, before_ref, piece_refs, out_ref):
    def use(line, total):
        out_ref[line] = total if before_ref is None else before_ref[line] + total

    each_line(groups, size, pairs, places, lhs_ref, bias_ref, piece_refs, use)


def add_kernel(groups, size, pairs, places, lhs_ref, bias_ref, before_ref, *refs):
    add_pieces(
        groups, size, pairs, places, lhs_ref, bias_ref, before_ref, refs[:-1], refs[-1]
    )


def finish_kernel(
    heads, groups, size, pairs, place, lhs_ref, bias_ref, sums_ref, wv_ref, gate_ref, *refs
):
    piece_refs, far_refs = refs[:groups], refs[groups : 4 * groups]
    mine_ref, theirs_ref, turned_ref, range_ref, copy_ref = refs[4 * groups :]
    blocks = 2 * heads
    low = iota((lhs_ref.shape[1], 128), 1) < 64

    def settle(line, total):
        start = line * pairs
        if not isinstance(line, int):
            start = pl.multiple_of(start, pairs)
        total = total.astype(BF16)
        for n in range(2):
            for b in range(blocks):
                part = total[(n * blocks + b) * pairs : (n * blocks + b + 1) * pairs]
                turned_ref[n, pl.ds(start, pairs), b * 128 : (b + 1) * 128] = part

    lowest, highest = [], []

    def use(line, total):
        total = sums_ref[line] + total
        settle(line, total)
        weight = jnp.where(low, 1.0, total).reshape(-1, 8, 128)
        lowest.append(jnp.min(weight, axis=0))
        highest.append(jnp.max(weight, axis=0))

    each_line(groups, size, pairs, (place,) * groups, lhs_ref, bias_ref, piece_refs, use)
    range_ref[0] = functools.reduce(jnp.minimum, lowest)
    range_ref[1] = functools.reduce(jnp.maximum, highest)
    fine = (range_ref[0] > 2.0**-80) & (range_ref[1] < 2.0**100)

    @pl.when(jnp.min(jnp.where(fine, 1.0, 0.0)) < 0.5)
    def _():
        for n, ref in enumerate(far_refs):
            pltpu.sync_copy(ref, copy_ref.at[n])
        for g in range(groups):
            ordered = [copy_ref.at[n * groups + g] for n in range(3)] + [piece_refs[g]]
            all_masks = [masks_of(ref, size, pairs) for ref in ordered]

            def exact_line(s, carry):
                line = g * size + s
                both = [keys_of(r, m, s, size, pairs) for r, m in zip(ordered, all_masks)]
                logits = []
                for n, (keyed, _) in enumerate(both):
                    width = keyed.shape[0]
                    bias = bias_ref[:, n * width : (n + 1) * width]
                    logits.append(mm_nt(lhs_ref[line], keyed) + bias)
                peak = functools.reduce(jnp.maximum, logits)
                peak = jnp.max(peak, axis=-1, keepdims=True)
                parts = [
                    mm(jnp.exp2(part - peak).astype(BF16), valued)
                    for part, (_, valued) in zip(logits, both)
                ]
                settle(line, sum(parts[1:], parts[0]))
                return carry

            lax.fori_loop(0, size, exact_line, 0)

    lead = groups * size * pairs
    mixed = mm(turned_ref[...].reshape(2 * lead, blocks * 128), wv_ref[...])
    mixed = (mixed[:, :128] / mixed[:, 128:]).reshape(2, lead, 128)
    for n, out_ref in enumerate((mine_ref, theirs_ref)):
        out_ref[...] = (gate_ref[n] * mixed[n]).astype(BF16)


def final_kernel(
    lines, depth, with_column, me_ref, line_ref, kept_ref, w_ref, mine_ref, theirs_ref, out_ref,
    gated_ref,
):
    total = line_ref.shape[0]
    pairs = total // lines
    core = me_ref[0] % 2
    share = total // 2
    for owner, ref in ((core, mine_ref), (1 - core, theirs_ref)):
        gated_ref[pl.ds(pl.multiple_of(owner * share, share), share), :] = ref[...]
    row = (line_ref[...].astype(F32) + mm(gated_ref[...], w_ref[:, :128])).astype(BF16)
    if not with_column:
        out_ref[...] = row
        return
    kept = kept_ref[...]
    projected = mm(paired_norm(row, 64), w_ref[:, 256:])
    query, gate, key, value = [projected[:, 128 * n : 128 * (n + 1)] for n in range(4)]

    def grid(a):
        return a.reshape(lines, pairs, 128)

    count = jnp.maximum(jnp.sum(grid(kept), axis=0), 1.0)
    mean_query = jnp.sum(grid(kept * query), axis=0) / count * (depth**-0.5)
    same_head = block_matrix(128, depth, 1.0, 1.0)
    product = (mean_query[None] * grid(key)).reshape(total, 128)
    logits = grid(mm_split(product, same_head) + 1e9 * (kept - 1.0))
    exped = jnp.exp(logits - jnp.max(logits, axis=0, keepdims=True))
    mixed = jnp.sum(exped * grid(value), axis=0) / jnp.sum(exped, axis=0)
    gated = (jax.nn.sigmoid(grid(gate)) * mixed[None]).reshape(total, 128).astype(BF16)
    result = (row.astype(F32) + mm(gated, w_ref[:, 128:256])).astype(BF16)
    shuffled = row_shuffle(result, lines, pairs)
    for t in range(pairs):
        out_ref[:, t * 128 : (t + 1) * 128] = shuffled[t * lines : (t + 1) * lines, :]


def call(kernel, out_shape, *args, **options):
    flops = options.pop("flops", 0)
    limit = pltpu.CompilerParams(vmem_limit_bytes=options.pop("mib", 8) * 1024 * 1024)
    moved = sum(a.size * a.dtype.itemsize for a in args)
    cost = pl.CostEstimate(flops=flops, bytes_accessed=moved, transcendentals=0)
    return pl.pallas_call(
        kernel, out_shape=out_shape, compiler_params=limit, cost_estimate=cost, **options
    )(*args)


def shape(*dims, dtype=BF16):
    return jax.ShapeDtypeStruct(dims, dtype)


def exchange(x, flip, devices):
    return lax.ppermute(x, "res", [(d, d ^ flip) for d in range(devices)])


def layer_normalize(values_in):
    centre = values_in - jnp.mean(values_in, axis=-1, keepdims=True)
    spread = jnp.mean(centre * centre, axis=-1, keepdims=True)
    return centre * lax.rsqrt(spread + EPS)


def column_complete(line, kept, vertical_matrix, vertical_exit_matrix, heads, depth):
    lines, columns, features = line.shape
    hidden = heads * depth
    normed = layer_normalize(line.astype(F32)).astype(BF16)
    projected = mm(normed.reshape(-1, features), vertical_matrix).reshape(lines, columns, -1)
    query, gate = projected[..., :hidden], projected[..., hidden : 2 * hidden]
    key = projected[..., 2 * hidden : 2 * hidden + depth]
    value = projected[..., 2 * hidden + depth :]
    count = jnp.maximum(jnp.sum(kept, axis=0), 1.0)[:, None]
    mean_query = jnp.sum(kept[..., None] * query, axis=0) / count * depth**-0.5
    logits = jnp.einsum("ihc,sic->sih", mean_query.reshape(columns, heads, depth), key)
    logits = logits + 1e9 * (kept - 1.0)[..., None]
    exped = jnp.exp(logits - jnp.max(logits, axis=0, keepdims=True))
    mixed = jnp.einsum("sih,sic->ihc", exped, value) / jnp.sum(exped, axis=0)[..., None]
    gate = jax.nn.sigmoid(gate).reshape(lines, columns, heads, depth)
    gated = (gate * mixed[None]).reshape(-1, hidden).astype(BF16)
    update = mm(gated, vertical_exit_matrix).reshape(lines, columns, features)
    return (line.astype(F32) + update).astype(BF16)


def on_device(
    seq_size,
    res_size,
    extra_activations,
    pair,
    present,
    amino,
    offset_matrix,
    horizontal_matrix,
    horizontal_exit_matrix,
    vertical_matrix,
    vertical_exit_matrix,
):
    lines, residues = present.shape
    pairs = residues // 2
    hidden = horizontal_exit_matrix.shape[0]
    heads = offset_matrix.shape[1]
    depth = hidden // heads
    groups = 2
    size = lines // (2 * groups)
    lead = size * pairs
    keys = res_size * residues
    rows = residues * heads
    core_bit, near, far, high = 1, 2, 4, 8
    kept = (present * amino[None, :]).astype(BF16)
    me = lax.axis_index("res").astype(jnp.int32).reshape(1)
    smem = pl.BlockSpec(memory_space=pltpu.SMEM)
    vmem = pl.BlockSpec(memory_space=pltpu.VMEM)

    rest = lead + pairs
    keep, send, line = call(
        functools.partial(prep_kernel, groups),
        [shape(groups, rest, 128)] * 2 + [shape(lines * pairs, 128)],
        me,
        extra_activations,
        kept,
        in_specs=[smem, vmem, vmem],
        scratch_shapes=[
            pltpu.VMEM((lines * pairs, 128), BF16),
            pltpu.VMEM((2 * groups, pairs, 128), BF16),
        ],
    )

    received = exchange(send, core_bit, res_size)
    chunk = jnp.concatenate(
        [keep[:, :lead], received[:, :lead], keep[:, lead:] + received[:, lead:]], axis=1
    )
    levels = [chunk] + [exchange(chunk, high * k, res_size) for k in range(1, res_size // high)]
    own = [jnp.stack([level[g] for level in levels]) for g in range(groups)]
    beside = [exchange(part, near, res_size) for part in own]
    across = [exchange(part, far, res_size) for part in own]

    per_step = 8
    pieces = 4
    whole = seq_size == 1
    bias_rows = [shape(rows, keys)] * 2
    bias = call(
        functools.partial(bias_kernel, whole, pieces),
        bias_rows if whole else [shape(rows, pair.shape[1])],
        pair,
        offset_matrix.T,
        chunk,
        me,
        grid=(residues // per_step,),
        in_specs=[
            pl.BlockSpec((per_step,) + pair.shape[1:], lambda n: (n, 0, 0)),
            pl.BlockSpec(offset_matrix.shape[::-1], lambda n: (0, 0)),
            pl.BlockSpec(memory_space=pl.ANY),
            smem,
        ],
        out_specs=[pl.BlockSpec((rows, pair.shape[1]), lambda n: (0, 0))] * (1 + whole),
        scratch_shapes=[
            pltpu.VMEM((rows // 128, pair.shape[1], 128), F32),
            pltpu.VMEM((2 * pair.shape[2], 2 * pair.shape[2]), BF16),
            pltpu.VMEM((pair.shape[2], rows), F32),
        ],
        flops=16 * pair.size * 128,
        mib=57,
    )
    if not whole:
        bias = call(
            functools.partial(order_kernel, residues, pieces),
            bias_rows,
            me,
            lax.all_gather(bias[0], "seq", axis=1, tiled=True),
            in_specs=[smem, vmem],
            mib=14,
        )
    bias, lhs, sums, wv, gate, w_final, kept_wide = call(
        functools.partial(query_kernel, groups, size, pairs, heads),
        [
            shape(2 * rows, keys, dtype=F32),
            shape(groups * size, 2 * rows, 128),
            shape(groups * size, 2 * rows, 128, dtype=F32),
            shape(2 * heads * 128, 256),
            shape(2, groups * lead, 128, dtype=F32),
            shape(128, 6 * 128),
            shape(lines * pairs, 128, dtype=F32),
        ],
        bias[0],
        exchange(bias[1], core_bit, res_size),
        keep,
        received,
        horizontal_matrix,
        horizontal_exit_matrix,
        vertical_matrix,
        vertical_exit_matrix,
        kept,
        *own,
        in_specs=[vmem] * (9 + groups),
        flops=8 * rows * keys * keys,
        mib=20,
    )

    def add(sums, places, parts):
        return call(
            functools.partial(add_kernel, groups, size, pairs, places),
            shape(*sums.shape, dtype=F32),
            lhs,
            bias,
            sums,
            *parts,
            flops=groups * size * rows * keys * 2 * 256 * 2,
            mib=20,
        )

    beside[0], across[1], sums = lax.optimization_barrier((beside[0], across[1], sums))
    corner = [
        exchange(beside[g], far, res_size) if g % 2 == 0 else exchange(across[g], near, res_size)
        for g in range(groups)
    ]
    sums = add(sums, (1, 2), (beside[0], across[1]))
    beside[1], across[0], sums = lax.optimization_barrier((beside[1], across[0], sums))
    sums = add(sums, (2, 1), (across[0], beside[1]))
    corner[0], corner[1], sums = lax.optimization_barrier((corner[0], corner[1], sums))
    anywhere = pl.BlockSpec(memory_space=pl.ANY)
    mine, theirs = call(
        functools.partial(finish_kernel, heads, groups, size, pairs, 3),
        [shape(groups * lead, 128)] * 2,
        lhs,
        bias,
        sums,
        wv,
        gate,
        *corner,
        *own,
        *beside,
        *across,
        in_specs=[vmem] * (5 + groups) + [anywhere] * (3 * groups),
        scratch_shapes=[
            pltpu.VMEM((2, groups * lead, 128 * 2 * heads), BF16),
            pltpu.VMEM((2, 8, 128), F32),
            pltpu.VMEM((3 * groups,) + own[0].shape, BF16),
        ],
        flops=groups * size * rows * keys * 2 * 256,
        mib=24,
    )
    returned = exchange(theirs, core_bit, res_size)
    with_column = seq_size == 1
    final_args = [
        me,
        line,
        kept_wide,
        w_final,
    ]
    final_args += [mine, returned]
    result = call(
        functools.partial(final_kernel, lines, depth, with_column),
        shape(*extra_activations.shape) if with_column else shape(lines * pairs, 128),
        *final_args,
        in_specs=[smem] + [vmem] * (len(final_args) - 1),
        scratch_shapes=[pltpu.VMEM((lines * pairs, 128), BF16)],
    )
    if with_column:
        return result
    row = result.reshape(lines, residues, hidden)
    moved = lax.all_to_all(row, "seq", split_axis=1, concat_axis=0, tiled=True)
    moved_kept = lax.all_to_all(kept, "seq", split_axis=1, concat_axis=0, tiled=True)
    updated = column_complete(
        moved, moved_kept.astype(F32), vertical_matrix, vertical_exit_matrix, heads, depth
    )
    back = lax.all_to_all(updated, "seq", split_axis=0, concat_axis=1, tiled=True)
    return back.reshape(extra_activations.shape)


def solution(mesh):
    in_specs = (
        P("seq", "res"),
        P("res", "seq", None),
        P("seq", "res"),
        P("res"),
        P(),
        P(),
        P(),
        P(),
        P(),
    )
    sizes = mesh.shape
    return jax.shard_map(
        functools.partial(on_device, sizes["seq"], sizes["res"]),
        mesh=mesh,
        in_specs=in_specs,
        out_specs=P("seq", "res"),
        check_vma=False,
    )
```

profile of v0, /device:TPU:0, one launch (start us, length us, event | category | flops | bytes accessed | tf_op | source)
XLA Modules:
  0.0 73.4 jit_solution(17259753620715572684)
XLA Ops:
  0.0 0.7 multiply_convert_fusion.kept_ref
  0.7 0.9 %copy-done = bf16[32,2048]{1,0:T(8,128)(2,1)S(1)} copy-done((bf16[32,2048]{1,0:T(8,128)(2,1)S(1)}, bf16[32,2048]{1,0:T(8,128)(2,1)}, u32[]{:S(2)}) %copy-start) | copy-done | bytes 131096
  1.6 1.2 %shard_map.91 = (bf16[2,144,128]{2,1,0:T(8,128)(2,1)S(1)}, bf16[2,144,128]{2,1,0:T(8,128)(2,1)S(1)}, bf16[512,128]{1,0:T(8,128)(2,1)S(1)}) custom-call(s32[1]{0:T(128)} %bitcast.me_ref, bf16[32,2048]{1,0:T(8,128)(2,1)S(1)} %copy-done, bf16[32,32]{1,0:T(8,128)(2,1)S(1)} %multiply_convert_fusion.kept_ref), custom_call_target="tpu_custom_call" | custom-call | bytes 133124 | tf_op jit(solution)/shard_map/pallas_call | solution.py:437
  2.8 0.5 collective-permute-start
  3.3 0.9 %collective-permute-done.received_ref = bf16[2,144,128]{2,1,0:T(8,128)(2,1)S(1)} collective-permute-done((bf16[2,144,128]{2,1,0:T(8,128)(2,1)S(1)}, bf16[2,144,128]{2,1,0:T(8,128)(2,1)S(1)}, u32[]{:S(2)}, u32[]{:S(2)}) %collective-permute-start) | collective-permute-done | bytes 73760 | tf_op jit(solution)/shard_map/ppermute | solution.py:447
  4.3 5.0 %collective-permute-start.4 = (bf16[2,272,128]{2,1,0:T(8,128)(2,1)S(1)}, bf16[2,272,128]{2,1,0:T(8,128)(2,1)S(1)}, u32[]{:S(2)}, u32[]{:S(2)}) collective-permute-start(bf16[2,272,128]{2,1,0:T(8,128)(2,1)S(1)} %pad_maximum_fusion.2.after_ref), channel_id=1, source_target_pairs={{0,24},{1,25},{2,26},{3,27},{4,28},{5,29},{6,30},{7,31},{8,16},{9,... | collective-permute-start | bytes 417800 | tf_op jit(solution)/shard_map/ppermute | solution.py:447
  9.3 0.0 collective-permute-start.3
  9.3 0.6 collective-permute-start.2
  10.0 0.0 copy-start.4
  10.0 9.2 %shard_map.92 = (bf16[256,1024]{1,0:T(8,128)(2,1)}, bf16[256,1024]{1,0:T(8,128)(2,1)}) custom-call(bf16[32,1024,128]{2,1,0:T(8,128)(2,1)} %x_ref.1, bf16[8,128]{1,0:T(8,128)(2,1)} %bitcast.2, bf16[2,272,128]{2,1,0:T(8,128)(2,1)} %copy-done.6, s32[1]{0:T(128)} %bitcast.me_ref), custom_call_target="tpu_custom_call" | custom-call | flops 8589934592 | bytes 8529924 | tf_op jit(solution)/shard_map/pallas_call | solution.py:437
  19.2 0.9 %fusion = (bf16[1,272,128]{2,1,0:T(8,128)(2,1)S(1)}, bf16[1,272,128]{2,1,0:T(8,128)(2,1)S(1)}) fusion(bf16[2,272,128]{2,1,0:T(8,128)(2,1)} %copy-done.6), kind=kLoop, calls=%fused_computation.5 | loop fusion | bytes 278528 | tf_op jit(solution)/shard_map/slice | solution.py:524
  20.1 0.0 collective-permute-done.4
  20.2 1.2 %collective-permute-done.3 = bf16[2,272,128]{2,1,0:T(8,128)(2,1)S(1)} collective-permute-done((bf16[2,272,128]{2,1,0:T(8,128)(2,1)S(1)}, bf16[2,272,128]{2,1,0:T(8,128)(2,1)S(1)}, u32[]{:S(2)}, u32[]{:S(2)}) %collective-permute-start.3) | collective-permute-done | bytes 139296 | tf_op jit(solution)/shard_map/ppermute | solution.py:447
  21.5 1.6 %collective-permute-start.5 = (bf16[4,272,128]{2,1,0:T(8,128)(2,1)S(1)}, bf16[4,272,128]{2,1,0:T(8,128)(2,1)S(1)}, u32[]{:S(2)}, u32[]{:S(2)}) collective-permute-start(bf16[4,272,128]{2,1,0:T(8,128)(2,1)S(1)} %pad_maximum_fusion.refs_0_.refs_2_), channel_id=1, source_target_pairs={{0,2},{1,3},{2,0},{3,1},{4,6},{5,7},{6,4},{7,5},{8,10},{9,11},{10,... | collective-permute-start | bytes 835592 | tf_op jit(solution)/shard_map/ppermute | solution.py:447
  23.1 1.6 %collective-permute-start.6 = (bf16[4,272,128]{2,1,0:T(8,128)(2,1)S(1)}, bf16[4,272,128]{2,1,0:T(8,128)(2,1)S(1)}, u32[]{:S(2)}, u32[]{:S(2)}) collective-permute-start(bf16[4,272,128]{2,1,0:T(8,128)(2,1)S(1)} %pad_maximum_fusion.1.refs_1_.refs_3_), channel_id=1, source_target_pairs={{0,4},{1,5},{2,6},{3,7},{4,0},{5,1},{6,2},{7,3},{8,12},{9,13},{10,... | collective-permute-start | bytes 835592 | tf_op jit(solution)/shard_map/ppermute | solution.py:447
  24.7 0.5 collective-permute-start.10
  25.2 0.5 collective-permute-start.9
  25.7 1.0 %copy-done.5 = bf16[256,1024]{1,0:T(8,128)(2,1)S(1)} copy-done((bf16[256,1024]{1,0:T(8,128)(2,1)S(1)}, bf16[256,1024]{1,0:T(8,128)(2,1)}, u32[]{:S(2)}) %copy-start.5) | copy-done | bytes 524312
  26.8 4.4 %shard_map.93 = (f32[512,1024]{1,0:T(8,128)S(1)}, bf16[16,512,128]{2,1,0:T(8,128)(2,1)S(1)}, f32[16,512,128]{2,1,0:T(8,128)S(1)}, bf16[2048,256]{1,0:T(8,128)(2,...) custom-call(bf16[256,1024]{1,0:T(8,128)(2,1)S(1)} %copy-done.5, ...), custom_call_target="tpu_custom_call" | custom-call | flops 2147483648 | bytes 1822720 | tf_op jit(solution)/shard_map/pallas_call | solution.py:437
  31.2 0.0 collective-permute-done.5.refs_0_.refs_4_
  31.2 1.5 %collective-permute-done.6.refs_1_.refs_7_ = bf16[4,272,128]{2,1,0:T(8,128)(2,1)S(1)} collective-permute-done((bf16[4,272,128]{2,1,0:T(8,128)(2,1)S(1)}, bf16[4,272,128]{2,1,0:T(8,128)(2,1)S(1)}, u32[]{:S(2)}, u32[]{:S(2)}) %collective-permute-start.6) | collective-permute-done | bytes 278560 | tf_op jit(solution)/shard_map/ppermute | solution.py:447
  32.7 1.5 %collective-permute-start.7 = (bf16[4,272,128]{2,1,0:T(8,128)(2,1)S(1)}, bf16[4,272,128]{2,1,0:T(8,128)(2,1)S(1)}, u32[]{:S(2)}, u32[]{:S(2)}) collective-permute-start(bf16[4,272,128]{2,1,0:T(8,128)(2,1)S(1)} %collective-permute-done.5.refs_0_.refs_4_), channel_id=1, source_target_pairs={{0,4},{1,5},{2,6},{3,7},{4,0},{5,1},{6,2},{7,3},{8,12},{9,13},{10,... | collective-permute-start | bytes 835592 | tf_op jit(solution)/shard_map/ppermute | solution.py:447
  34.3 0.5 collective-permute-start.8
  34.8 2.6 %shard_map.94.before_ref = f32[16,512,128]{2,1,0:T(8,128)S(1)} custom-call(bf16[16,512,128]{2,1,0:T(8,128)(2,1)S(1)} %get-tuple-element.35.lhs_ref, f32[512,1024]{1,0:T(8,128)S(1)} %get-tuple-element.36.bias_ref, f32[16,512,128]{2,1,0:T(8,128)S(1)} %get-tuple-element.40.before_ref, bf16[4,272,128]{2,1,0:T(8,128)(2,1)S(1)} %collective-permute-done.5.refs_0_.refs_4_, ...), custom_call_target="tpu_custom_call" | custom-call | flops 4294967296 | bytes 8945664 | tf_op jit(solution)/shard_map/pallas_call | solution.py:437
  37.4 1.3 %collective-permute-done.10.refs_0_.refs_6_ = bf16[4,272,128]{2,1,0:T(8,128)(2,1)S(1)} collective-permute-done((bf16[4,272,128]{2,1,0:T(8,128)(2,1)S(1)}, bf16[4,272,128]{2,1,0:T(8,128)(2,1)S(1)}, u32[]{:S(2)}, u32[]{:S(2)}) %collective-permute-start.10) | collective-permute-done | bytes 278560 | tf_op jit(solution)/shard_map/ppermute | solution.py:447
  38.7 0.0 collective-permute-done.9.refs_1_.refs_5_
  38.7 2.4 %shard_map.95.sums_ref = f32[16,512,128]{2,1,0:T(8,128)S(1)} custom-call(bf16[16,512,128]{2,1,0:T(8,128)(2,1)S(1)} %get-tuple-element.35.lhs_ref, f32[512,1024]{1,0:T(8,128)S(1)} %get-tuple-element.36.bias_ref, f32[16,512,128]{2,1,0:T(8,128)S(1)} %shard_map.94.before_ref, bf16[4,272,128]{2,1,0:T(8,128)(2,1)S(1)} %collective-permute-done.10.refs_0_.refs_6_, ...), custom_call_target="tpu_custom_call" | custom-call | flops 4294967296 | bytes 8945664 | tf_op jit(solution)/shard_map/pallas_call | solution.py:437
  41.2 1.7 %collective-permute-done.7.refs_0_ = bf16[4,272,128]{2,1,0:T(8,128)(2,1)S(1)} collective-permute-done((bf16[4,272,128]{2,1,0:T(8,128)(2,1)S(1)}, bf16[4,272,128]{2,1,0:T(8,128)(2,1)S(1)}, u32[]{:S(2)}, u32[]{:S(2)}) %collective-permute-start.7) | collective-permute-done | bytes 278560 | tf_op jit(solution)/shard_map/ppermute | solution.py:447
  42.8 27.0 %shard_map.96 = (bf16[256,128]{1,0:T(8,128)(2,1)S(1)}, bf16[256,128]{1,0:T(8,128)(2,1)S(1)}) custom-call(bf16[16,512,128]{2,1,0:T(8,128)(2,1)S(1)} %get-tuple-element.35.lhs_ref, f32[512,1024]{1,0:T(8,128)S(1)} %get-tuple-element.36.bias_ref, f32[16,512,128]{2,1,0:T(8,128)S(1)} %shard_map.95.sums_ref, bf16[2048,256]{1,0:T(8,128)(2,1)S(1)} %get-tuple-element.45.wv_ref, ...), custom_call_target="tpu_custom_call" | custom-call | flops 2147483648 | bytes 11927552 | tf_op jit(solution)/shard_map/pallas_call | solution.py:437
  69.8 0.1 collective-permute-start.11
  69.9 1.2 %collective-permute-done.11.theirs_ref = bf16[256,128]{1,0:T(8,128)(2,1)S(1)} collective-permute-done((bf16[256,128]{1,0:T(8,128)(2,1)S(1)}, bf16[256,128]{1,0:T(8,128)(2,1)S(1)}, u32[]{:S(2)}, u32[]{:S(2)}) %collective-permute-start.11) | collective-permute-done | bytes 65568 | tf_op jit(solution)/shard_map/ppermute | solution.py:447
  71.1 2.3 %shard_map.97 = bf16[32,2048]{1,0:T(8,128)(2,1)} custom-call(s32[1]{0:T(128)} %bitcast.me_ref, bf16[512,128]{1,0:T(8,128)(2,1)S(1)} %get-tuple-element.28.line_ref, f32[512,128]{1,0:T(8,128)S(1)} %get-tuple-element.33.kept_ref, bf16[128,768]{1,0:T(8,128)(2,1)S(1)} %get-tuple-element.34.w_ref, bf16[256,128]{1,0:T(8,128)(2,1)S(1)} %get-tuple-element.49.mine_ref, ...), custom_call_target="tpu_custom_call" | custom-call | bytes 720900 | tf_op jit(solution)/shard_map/pallas_call | solution.py:437
  (24 shorter events, 0.2 us)
Async XLA Ops:
  0.7 0.9 %copy-start = (bf16[32,2048]{1,0:T(8,128)(2,1)S(1)}, bf16[32,2048]{1,0:T(8,128)(2,1)}, u32[]{:S(2)}) copy-start(bf16[32,2048]{1,0:T(8,128)(2,1)} %m_ref.1) | copy-start | bytes 393220
  2.8 1.4 %collective-permute-start = (bf16[2,144,128]{2,1,0:T(8,128)(2,1)S(1)}, bf16[2,144,128]{2,1,0:T(8,128)(2,1)S(1)}, u32[]{:S(2)}, u32[]{:S(2)}) collective-permute-start(bf16[2,144,128]{2,1,0:T(8,128)(2,1)S(1)} %get-tuple-element.30), channel_id=1, source_target_pairs={{0,1},{1,0},{2,3},{3,2},{4,5},{5,4},{6,7},{7,6},{8,9},{9,8},{10,11... | collective-permute-start | bytes 221192 | tf_op jit(solution)/shard_map/ppermute | solution.py:447
  4.3 5.7 %copy-start.6 = (bf16[2,272,128]{2,1,0:T(8,128)(2,1)}, bf16[2,272,128]{2,1,0:T(8,128)(2,1)S(1)}, u32[]{:S(2)}) copy-start(bf16[2,272,128]{2,1,0:T(8,128)(2,1)S(1)} %pad_maximum_fusion.2.after_ref) | copy-start | bytes 417796
  4.3 15.9 %collective-permute-start.4 = (bf16[2,272,128]{2,1,0:T(8,128)(2,1)S(1)}, bf16[2,272,128]{2,1,0:T(8,128)(2,1)S(1)}, u32[]{:S(2)}, u32[]{:S(2)}) collective-permute-start(bf16[2,272,128]{2,1,0:T(8,128)(2,1)S(1)} %pad_maximum_fusion.2.after_ref), channel_id=1, source_target_pairs={{0,24},{1,25},{2,26},{3,27},{4,28},{5,29},{6,30},{7,31},{8,16},{9,... | collective-permute-start | bytes 417800 | tf_op jit(solution)/shard_map/ppermute | solution.py:447
  9.3 12.1 %collective-permute-start.3 = (bf16[2,272,128]{2,1,0:T(8,128)(2,1)S(1)}, bf16[2,272,128]{2,1,0:T(8,128)(2,1)S(1)}, u32[]{:S(2)}, u32[]{:S(2)}) collective-permute-start(bf16[2,272,128]{2,1,0:T(8,128)(2,1)S(1)} %pad_maximum_fusion.2.after_ref), channel_id=1, source_target_pairs={{0,16},{1,17},{2,18},{3,19},{4,20},{5,21},{6,22},{7,23},{8,24},{9,... | collective-permute-start | bytes 417800 | tf_op jit(solution)/shard_map/ppermute | solution.py:447
  9.3 12.1 %collective-permute-start.2 = (bf16[2,272,128]{2,1,0:T(8,128)(2,1)S(1)}, bf16[2,272,128]{2,1,0:T(8,128)(2,1)S(1)}, u32[]{:S(2)}, u32[]{:S(2)}) collective-permute-start(bf16[2,272,128]{2,1,0:T(8,128)(2,1)S(1)} %pad_maximum_fusion.2.after_ref), channel_id=1, source_target_pairs={{0,8},{1,9},{2,10},{3,11},{4,12},{5,13},{6,14},{7,15},{8,0},{9,1},... | collective-permute-start | bytes 417800 | tf_op jit(solution)/shard_map/ppermute | solution.py:447
  9.9 15.8 %copy-start.1 = (bf16[64,256]{1,0:T(8,128)(2,1)S(1)}, bf16[64,256]{1,0:T(8,128)(2,1)}, u32[]{:S(2)}) copy-start(bf16[64,256]{1,0:T(8,128)(2,1)} %w_ref.1) | copy-start | bytes 98308
  9.9 15.8 %copy-start.2 = (bf16[64,144]{1,0:T(8,128)(2,1)S(1)}, bf16[64,144]{1,0:T(8,128)(2,1)}, u32[]{:S(2)}) copy-start(bf16[64,144]{1,0:T(8,128)(2,1)} %column_ref.1) | copy-start | bytes 55300
  9.9 15.8 %copy-start.3 = (bf16[64,64]{1,0:T(8,128)(2,1)S(1)}, bf16[64,64]{1,0:T(8,128)(2,1)}, u32[]{:S(2)}) copy-start(bf16[64,64]{1,0:T(8,128)(2,1)} %exit_ref.1) | copy-start | bytes 24580
  10.0 15.8 %copy-start.4 = (bf16[64,64]{1,0:T(8,128)(2,1)S(1)}, bf16[64,64]{1,0:T(8,128)(2,1)}, u32[]{:S(2)}) copy-start(bf16[64,64]{1,0:T(8,128)(2,1)} %column_exit_ref.1) | copy-start | bytes 24580
  19.2 6.5 %collective-permute-start.1 = (bf16[256,1024]{1,0:T(8,128)(2,1)}, bf16[256,1024]{1,0:T(8,128)(2,1)S(1)}, u32[]{:S(2)}, u32[]{:S(2)}) collective-permute-start(bf16[256,1024]{1,0:T(8,128)(2,1)} %get-tuple-element.32), channel_id=1, source_target_pairs={{0,1},{1,0},{2,3},{3,2},{4,5},{5,4},{6,7},{7,6},{8,9},{9,8},{10,11... | collective-permute-start | bytes 1572872 | tf_op jit(solution)/shard_map/ppermute | solution.py:447
  21.5 9.7 %collective-permute-start.5 = (bf16[4,272,128]{2,1,0:T(8,128)(2,1)S(1)}, bf16[4,272,128]{2,1,0:T(8,128)(2,1)S(1)}, u32[]{:S(2)}, u32[]{:S(2)}) collective-permute-start(bf16[4,272,128]{2,1,0:T(8,128)(2,1)S(1)} %pad_maximum_fusion.refs_0_.refs_2_), channel_id=1, source_target_pairs={{0,2},{1,3},{2,0},{3,1},{4,6},{5,7},{6,4},{7,5},{8,10},{9,11},{10,... | collective-permute-start | bytes 835592 | tf_op jit(solution)/shard_map/ppermute | solution.py:447
  23.1 9.7 %collective-permute-start.6 = (bf16[4,272,128]{2,1,0:T(8,128)(2,1)S(1)}, bf16[4,272,128]{2,1,0:T(8,128)(2,1)S(1)}, u32[]{:S(2)}, u32[]{:S(2)}) collective-permute-start(bf16[4,272,128]{2,1,0:T(8,128)(2,1)S(1)} %pad_maximum_fusion.1.refs_1_.refs_3_), channel_id=1, source_target_pairs={{0,4},{1,5},{2,6},{3,7},{4,0},{5,1},{6,2},{7,3},{8,12},{9,13},{10,... | collective-permute-start | bytes 835592 | tf_op jit(solution)/shard_map/ppermute | solution.py:447
  24.7 14.0 %collective-permute-start.10 = (bf16[4,272,128]{2,1,0:T(8,128)(2,1)S(1)}, bf16[4,272,128]{2,1,0:T(8,128)(2,1)S(1)}, u32[]{:S(2)}, u32[]{:S(2)}) collective-permute-start(bf16[4,272,128]{2,1,0:T(8,128)(2,1)S(1)} %pad_maximum_fusion.refs_0_.refs_2_), channel_id=1, source_target_pairs={{0,4},{1,5},{2,6},{3,7},{4,0},{5,1},{6,2},{7,3},{8,12},{9,13},{10,... | collective-permute-start | bytes 835592 | tf_op jit(solution)/shard_map/ppermute | solution.py:447
  25.2 13.5 %collective-permute-start.9 = (bf16[4,272,128]{2,1,0:T(8,128)(2,1)S(1)}, bf16[4,272,128]{2,1,0:T(8,128)(2,1)S(1)}, u32[]{:S(2)}, u32[]{:S(2)}) collective-permute-start(bf16[4,272,128]{2,1,0:T(8,128)(2,1)S(1)} %pad_maximum_fusion.1.refs_1_.refs_3_), channel_id=1, source_target_pairs={{0,2},{1,3},{2,0},{3,1},{4,6},{5,7},{6,4},{7,5},{8,10},{9,11},{10,... | collective-permute-start | bytes 835592 | tf_op jit(solution)/shard_map/ppermute | solution.py:447
  25.7 1.0 %copy-start.5 = (bf16[256,1024]{1,0:T(8,128)(2,1)S(1)}, bf16[256,1024]{1,0:T(8,128)(2,1)}, u32[]{:S(2)}) copy-start(bf16[256,1024]{1,0:T(8,128)(2,1)} %get-tuple-element.31.own_ref) | copy-start | bytes 1572868
  32.7 10.1 %collective-permute-start.7 = (bf16[4,272,128]{2,1,0:T(8,128)(2,1)S(1)}, bf16[4,272,128]{2,1,0:T(8,128)(2,1)S(1)}, u32[]{:S(2)}, u32[]{:S(2)}) collective-permute-start(bf16[4,272,128]{2,1,0:T(8,128)(2,1)S(1)} %collective-permute-done.5.refs_0_.refs_4_), channel_id=1, source_target_pairs={{0,4},{1,5},{2,6},{3,7},{4,0},{5,1},{6,2},{7,3},{8,12},{9,13},{10,... | collective-permute-start | bytes 835592 | tf_op jit(solution)/shard_map/ppermute | solution.py:447
  34.3 8.6 %collective-permute-start.8 = (bf16[4,272,128]{2,1,0:T(8,128)(2,1)S(1)}, bf16[4,272,128]{2,1,0:T(8,128)(2,1)S(1)}, u32[]{:S(2)}, u32[]{:S(2)}) collective-permute-start(bf16[4,272,128]{2,1,0:T(8,128)(2,1)S(1)} %collective-permute-done.6.refs_1_.refs_7_), channel_id=1, source_target_pairs={{0,2},{1,3},{2,0},{3,1},{4,6},{5,7},{6,4},{7,5},{8,10},{9,11},{10,... | collective-permute-start | bytes 835592 | tf_op jit(solution)/shard_map/ppermute | solution.py:447
  69.8 1.3 %collective-permute-start.11 = (bf16[256,128]{1,0:T(8,128)(2,1)S(1)}, bf16[256,128]{1,0:T(8,128)(2,1)S(1)}, u32[]{:S(2)}, u32[]{:S(2)}) collective-permute-start(bf16[256,128]{1,0:T(8,128)(2,1)S(1)} %get-tuple-element.50), channel_id=1, source_target_pairs={{0,1},{1,0},{2,3},{3,2},{4,5},{5,4},{6,7},{7,6},{8,9},{9,8},{10,11... | collective-permute-start | bytes 196616 | tf_op jit(solution)/shard_map/ppermute | solution.py:447
where the time goes:
time: 73.8 us; the launch traced here: 73.4 us
  Pallas kernels  49.2 us (67%)
  starting transfers between devices  12.4 us (17%)
  waiting for transfers between devices  7.9 us (11%)
  local copies, waits for them, and re-layouts  2.93 us (4%)
  other arithmetic  0.82 us (1%)
    pallas_call x7, Pallas kernels, call(): pl.pallas_call(kernel, out_shape=out_shape, compiler_params=limit, cost_e...  49.2 us
    ppermute x12, starting transfers between devices, exchange(): return lax.ppermute(x, 'res', [(d, d ^ flip) for d in range(devices)])  12.4 us
    ppermute x12, waiting for transfers between devices, exchange(): return lax.ppermute(x, 'res', [(d, d ^ flip) for d in range(devices)])  7.9 us
    unnamed x14, local copies, waits for them, and re-layouts  1.96 us
  transfers between devices with their start and end apart: 12, of which 6 were waited for; matrix products, arithmetic and copies ran while one was open for 1% of the time, Pallas kernels for 25%

commit v1 on v0

--- a/solution.py
+++ b/solution.py
@@ -91,12 +91,11 @@
             ref[g, rows:] = spread_ref[index]
 
 
-def bias_kernel(whole, pieces, x_ref, w_ref, after_ref, me_ref, *refs):
+def bias_kernel(whole, pieces, residues, x_ref, w_ref, after_ref, me_ref, *refs):
     outs, (acc_ref, centring_ref, wide_ref) = refs[:-3], refs[-3:]
     step = pl.program_id(0)
     heads = w_ref.shape[0]
-    per_step, keys, channels = x_ref.shape
-    residues = per_step * pl.num_programs(0)
+    per_step, _, keys, channels = x_ref.shape
     pairs = residues // 2
     tiles = acc_ref.shape[0]
     width = tiles * 128
@@ -106,17 +105,16 @@
         centring_ref[...] = block_matrix(
             2 * channels, channels, 1.0 - 1.0 / channels, -1.0 / channels
         )
-        spread = one_hot(iota((heads, 1), 0) == iota((1, width), 1) // residues)
+        spread = one_hot(iota((heads, 1), 0) == iota((1, width), 1) // pairs)
         wide_ref[...] = lax.dot_general(
             w_ref[...], spread, (((0,), (0,)), ((), ())), preferred_element_type=F32
         )
         acc_ref[...] = jnp.zeros(acc_ref.shape, F32)
 
-    lane = iota((1, width), 1) % residues
+    lane = iota((1, width), 1) % pairs
     placed = []
     for n in range(per_step):
-        residue = step * per_step + n
-        mine = lane == (residue % 2) * pairs + residue // 2
+        mine = lane == step * per_step + n
         placed.append(jnp.where(mine, wide_ref[...], 0.0).astype(BF16))
     placed = jnp.concatenate(placed, axis=0)
     centring = centring_ref[...]
@@ -124,7 +122,9 @@
     for r in range(0, keys, piece):
         normed = []
         for n in range(0, per_step, 2):
-            x = jnp.concatenate([x_ref[n, r : r + piece], x_ref[n + 1, r : r + piece]], axis=1)
+            x = jnp.concatenate(
+                [x_ref[n, 0, r : r + piece], x_ref[n + 1, 0, r : r + piece]], axis=1
+            )
             centre = mm(x, centring)
             for part in (centre[:, :channels], centre[:, channels:]):
                 spread = jnp.mean(part * part, axis=-1, keepdims=True)
@@ -198,20 +198,21 @@
     owner = col % 128 // depth
     return [
         jnp.where(owner == p * heads + h, wv, 0.0).astype(BF16)
+        for p in range(2)
         for h in range(heads)
-        for p in range(2)
     ]
 
 
 def query_kernel(
-    groups, size, pairs, heads, own_ref, peer_ref, keep_ref, received_ref, w_ref, exit_ref,
-    column_ref, column_exit_ref, kept_ref, *refs
+    groups, size, pairs, heads, even_ref, odd_ref, peer_even_ref, peer_odd_ref, keep_ref,
+    received_ref, w_ref, exit_ref, column_ref, column_exit_ref, kept_ref, *refs
 ):
     column_refs = refs[:groups]
     bias_ref, lhs_ref, sums_ref, wv_ref, gate_ref, final_ref, kept_wide_ref = refs[groups:]
-    rows = own_ref.shape[0]
-    bias_ref[:rows, :] = own_ref[...].astype(F32) * LOG2E
-    bias_ref[rows:, :] = peer_ref[...].astype(F32) * LOG2E
+    rows = 2 * even_ref.shape[0]
+    for n, ref in enumerate((even_ref, odd_ref, peer_even_ref, peer_odd_ref)):
+        at = slice(n * rows // 2, (n + 1) * rows // 2)
+        bias_ref[at, :] = ref[...].astype(F32) * LOG2E
 
     hidden = w_ref.shape[0]
     depth = hidden // heads
@@ -248,8 +249,8 @@
                 q = query[s * pairs : (s + 1) * pairs]
                 spread = [
                     jnp.where(lane // depth == p * heads + h, q, 0.0).astype(BF16)
+                    for p in range(2)
                     for h in range(heads)
-                    for p in range(2)
                 ]
                 folded = mm(jnp.concatenate(spread, axis=0), wk) * LOG2E
                 picks = (spare >= 0) & (spare < 4 * size) & (spare % size == s)
@@ -432,7 +433,7 @@
 def call(kernel, out_shape, *args, **options):
     flops = options.pop("flops", 0)
     limit = pltpu.CompilerParams(vmem_limit_bytes=options.pop("mib", 8) * 1024 * 1024)
-    moved = sum(a.size * a.dtype.itemsize for a in args)
+    moved = options.pop("moved", sum(a.size * a.dtype.itemsize for a in args))
     cost = pl.CostEstimate(flops=flops, bytes_accessed=moved, transcendentals=0)
     return pl.pallas_call(
         kernel, out_shape=out_shape, compiler_params=limit, cost_estimate=cost, **options
@@ -517,50 +518,68 @@
     )
 
     received = exchange(send, core_bit, res_size)
-    chunk = jnp.concatenate(
-        [keep[:, :lead], received[:, :lead], keep[:, lead:] + received[:, lead:]], axis=1
-    )
-    levels = [chunk] + [exchange(chunk, high * k, res_size) for k in range(1, res_size // high)]
-    own = [jnp.stack([level[g] for level in levels]) for g in range(groups)]
-    beside = [exchange(part, near, res_size) for part in own]
-    across = [exchange(part, far, res_size) for part in own]
+    chunks = [
+        jnp.concatenate([keep[g, :lead], received[g, :lead], keep[g, lead:] + received[g, lead:]])
+        for g in range(groups)
+    ]
 
     per_step = 8
     pieces = 4
     whole = seq_size == 1
-    bias_rows = [shape(rows, keys)] * 2
-    bias = call(
-        functools.partial(bias_kernel, whole, pieces),
-        bias_rows if whole else [shape(rows, pair.shape[1])],
-        pair,
-        offset_matrix.T,
-        chunk,
-        me,
-        grid=(residues // per_step,),
-        in_specs=[
-            pl.BlockSpec((per_step,) + pair.shape[1:], lambda n: (n, 0, 0)),
-            pl.BlockSpec(offset_matrix.shape[::-1], lambda n: (0, 0)),
-            pl.BlockSpec(memory_space=pl.ANY),
-            smem,
-        ],
-        out_specs=[pl.BlockSpec((rows, pair.shape[1]), lambda n: (0, 0))] * (1 + whole),
-        scratch_shapes=[
-            pltpu.VMEM((rows // 128, pair.shape[1], 128), F32),
-            pltpu.VMEM((2 * pair.shape[2], 2 * pair.shape[2]), BF16),
-            pltpu.VMEM((pair.shape[2], rows), F32),
-        ],
-        flops=16 * pair.size * 128,
-        mib=57,
-    )
+    by_parity = pair.reshape((residues // 2, 2) + pair.shape[1:])
+
+    def bias_of(parity, after):
+        return call(
+            functools.partial(bias_kernel, whole, pieces, residues),
+            [shape(rows // 2, pair.shape[1])] * (1 + whole),
+            by_parity,
+            offset_matrix.T,
+            after,
+            me,
+            grid=(residues // 2 // per_step,),
+            in_specs=[
+                pl.BlockSpec((per_step, 1) + pair.shape[1:], lambda n: (n, parity, 0, 0)),
+                pl.BlockSpec(offset_matrix.shape[::-1], lambda n: (0, 0)),
+                pl.BlockSpec(memory_space=pl.ANY),
+                smem,
+            ],
+            out_specs=[pl.BlockSpec((rows // 2, pair.shape[1]), lambda n: (0, 0))] * (1 + whole),
+            scratch_shapes=[
+                pltpu.VMEM((rows // 256, pair.shape[1], 128), F32),
+                pltpu.VMEM((2 * pair.shape[2], 2 * pair.shape[2]), BF16),
+                pltpu.VMEM((pair.shape[2], rows // 2), F32),
+            ],
+            flops=8 * pair.size * 128,
+            mib=48,
+        )
+
+    def levels_of(chunk):
+        return [chunk] + [exchange(chunk, high * k, res_size) for k in range(1, res_size // high)]
+
+    levels = levels_of(chunks[0])
+    bias = [bias_of(0, chunks[0])]
+    levels, bias[0] = lax.optimization_barrier((levels, bias[0]))
+    own = [jnp.stack(levels)]
+    own[0], later = lax.optimization_barrier((own[0], chunks[1]))
+    beside, across = [exchange(own[0], near, res_size)], [exchange(own[0], far, res_size)]
+    levels = levels_of(later)
+    bias.append(bias_of(1, own[0]))
+    levels, bias[1] = lax.optimization_barrier((levels, bias[1]))
+    own.append(jnp.stack(levels))
+    across.append(exchange(own[1], far, res_size))
+    beside.append(exchange(own[1], near, res_size))
     if not whole:
-        bias = call(
-            functools.partial(order_kernel, residues, pieces),
-            bias_rows,
-            me,
-            lax.all_gather(bias[0], "seq", axis=1, tiled=True),
-            in_specs=[smem, vmem],
-            mib=14,
-        )
+        bias = [
+            call(
+                functools.partial(order_kernel, residues, pieces),
+                [shape(rows // 2, keys)] * 2,
+                me,
+                lax.all_gather(part[0], "seq", axis=1, tiled=True),
+                in_specs=[smem, vmem],
+                mib=14,
+            )
+            for part in bias
+        ]
     bias, lhs, sums, wv, gate, w_final, kept_wide = call(
         functools.partial(query_kernel, groups, size, pairs, heads),
         [
@@ -572,8 +591,8 @@
             shape(128, 6 * 128),
             shape(lines * pairs, 128, dtype=F32),
         ],
-        bias[0],
-        exchange(bias[1], core_bit, res_size),
+        *[part[0] for part in bias],
+        *[exchange(part[1], core_bit, res_size) for part in bias],
         keep,
         received,
         horizontal_matrix,
@@ -582,8 +601,8 @@
         vertical_exit_matrix,
         kept,
         *own,
-        in_specs=[vmem] * (9 + groups),
-        flops=8 * rows * keys * keys,
+        in_specs=[vmem] * (11 + groups),
+        moved=0,
         mib=20,
     )
 
@@ -599,13 +618,14 @@
             mib=20,
         )
 
-    beside[0], across[1], sums = lax.optimization_barrier((beside[0], across[1], sums))
+    beside[0], across[0], across[1], sums = lax.optimization_barrier(
+        (beside[0], across[0], across[1], sums)
+    )
     corner = [
         exchange(beside[g], far, res_size) if g % 2 == 0 else exchange(across[g], near, res_size)
         for g in range(groups)
     ]
     sums = add(sums, (1, 2), (beside[0], across[1]))
-    beside[1], across[0], sums = lax.optimization_barrier((beside[1], across[0], sums))
     sums = add(sums, (2, 1), (across[0], beside[1]))
     corner[0], corner[1], sums = lax.optimization_barrier((corner[0], corner[1], sums))
     anywhere = pl.BlockSpec(memory_space=pl.ANY)

time: 73.8 us -> 77.2 us (1.046)
  starting transfers between devices: 12.4 us -> 18.5 us
  waiting for transfers between devices: 7.9 us -> 5 us
  Pallas kernels: 49.2 us -> 50.7 us
  local copies, waits for them, and re-layouts: 2.93 us -> 1.62 us
    ppermute x12 -> x16, starting transfers between devices: 12.4 us -> 18.5 us  [exchange(): return lax.ppermute(x, 'res', [(d, d ^ flip) for d in range(devices)])]
    ppermute x12 -> x16, waiting for transfers between devices: 7.9 us -> 5 us  [exchange(): return lax.ppermute(x, 'res', [(d, d ^ flip) for d in range(devices)])]
    pallas_call x7 -> x8, Pallas kernels: 49.2 us -> 50.7 us  [call(): pl.pallas_call(kernel, out_shape=out_shape, compiler_params=limit, cost_e...]
    slice x6 -> x0, local copies, waits for them, and re-layouts: 0.97 us -> none  [the longest x4 0.96 us: on_device(): own = [jnp.stack([level[g] for level in levels]) for g in range(groups)]]
  transfers between devices with their start and end apart: 12 -> 16, of which waited for: 6 -> 5; matrix products, arithmetic and copies ran while one was open for 1% -> 0% of each run, Pallas kernels for 25% -> 27%
where the time goes in v1:
time: 77.2 us; the launch traced here: 76.9 us
  Pallas kernels  50.7 us (66%)
  starting transfers between devices  18.5 us (24%)
  waiting for transfers between devices  5 us (6%)
  local copies, waits for them, and re-layouts  1.62 us (2%)
  other arithmetic  0.82 us (1%)
    pallas_call x8, Pallas kernels, call(): pl.pallas_call(kernel, out_shape=out_shape, compiler_params=limit, cost_e...  50.7 us
    ppermute x16, starting transfers between devices, exchange(): return lax.ppermute(x, 'res', [(d, d ^ flip) for d in range(devices)])  18.5 us
    ppermute x16, waiting for transfers between devices, exchange(): return lax.ppermute(x, 'res', [(d, d ^ flip) for d in range(devices)])  5 us
    unnamed x14, local copies, waits for them, and re-layouts  1.61 us
  transfers between devices with their start and end apart: 16, of which 5 were waited for; matrix products, arithmetic and copies ran while one was open for 0% of the time, Pallas kernels for 27%

profile of v1, /device:TPU:0, one launch (start us, length us, event | category | flops | bytes accessed | tf_op | source)
XLA Modules:
  0.0 76.9 jit_solution(1856121946810088391)
XLA Ops:
  0.0 0.7 multiply_convert_fusion.kept_ref
  0.7 0.9 %copy-done = bf16[32,2048]{1,0:T(8,128)(2,1)S(1)} copy-done((bf16[32,2048]{1,0:T(8,128)(2,1)S(1)}, bf16[32,2048]{1,0:T(8,128)(2,1)}, u32[]{:S(2)}) %copy-start) | copy-done | bytes 131096
  1.6 1.2 %shard_map.91 = (bf16[2,144,128]{2,1,0:T(8,128)(2,1)S(1)}, bf16[2,144,128]{2,1,0:T(8,128)(2,1)S(1)}, bf16[512,128]{1,0:T(8,128)(2,1)S(1)}) custom-call(s32[1]{0:T(128)} %bitcast.me_ref, bf16[32,2048]{1,0:T(8,128)(2,1)S(1)} %copy-done, bf16[32,32]{1,0:T(8,128)(2,1)S(1)} %multiply_convert_fusion.kept_ref), custom_call_target="tpu_custom_call" | custom-call | bytes 133124 | tf_op jit(solution)/shard_map/pallas_call | solution.py:438
  2.8 0.5 collective-permute-start
  3.3 0.9 %collective-permute-done.received_ref = bf16[2,144,128]{2,1,0:T(8,128)(2,1)S(1)} collective-permute-done((bf16[2,144,128]{2,1,0:T(8,128)(2,1)S(1)}, bf16[2,144,128]{2,1,0:T(8,128)(2,1)S(1)}, u32[]{:S(2)}, u32[]{:S(2)}) %collective-permute-start) | collective-permute-done | bytes 73760 | tf_op jit(solution)/shard_map/ppermute | solution.py:448
  4.3 5.0 %collective-permute-start.3 = (bf16[272,128]{1,0:T(8,128)(2,1)S(1)}, bf16[272,128]{1,0:T(8,128)(2,1)S(1)}, u32[]{:S(2)}, u32[]{:S(2)}) collective-permute-start(bf16[272,128]{1,0:T(8,128)(2,1)S(1)} %pad_maximum_fusion.2.after_ref), channel_id=1, source_target_pairs={{0,24},{1,25},{2,26},{3,27},{4,28},{5,29},{6,30},{7,31},{8,16},{9,... | collective-permute-start | bytes 208904 | tf_op jit(solution)/shard_map/ppermute | solution.py:448
  9.3 0.6 collective-permute-start.1
  9.9 0.7 copy-done.5
  10.6 5.5 %shard_map.92 = (bf16[128,1024]{1,0:T(8,128)(2,1)S(1)}, bf16[128,1024]{1,0:T(8,128)(2,1)S(1)}) custom-call(bf16[16,2,1024,128]{3,2,1,0:T(8,128)(2,1)} %bitcast.33, bf16[8,128]{1,0:T(8,128)(2,1)S(1)} %bitcast.24, bf16[272,128]{1,0:T(8,128)(2,1)S(1)} %pad_maximum_fusion.2.after_ref, s32[1]{0:T(128)} %bitcast.me_ref), custom_call_target="tpu_custom_call" | custom-call | flops 4294967296 | bytes 8460292 | tf_op jit(solution)/shard_map/pallas_call | solution.py:438
  16.2 0.0 copy-start.1
  16.2 0.0 copy-start.3
  16.2 0.0 copy-start.4
  16.2 3.8 %collective-permute-start.6 = (bf16[272,128]{1,0:T(8,128)(2,1)S(1)}, bf16[272,128]{1,0:T(8,128)(2,1)S(1)}, u32[]{:S(2)}, u32[]{:S(2)}) collective-permute-start(bf16[272,128]{1,0:T(8,128)(2,1)S(1)} %pad_maximum_fusion.3), channel_id=1, source_target_pairs={{0,24},{1,25},{2,26},{3,27},{4,28},{5,29},{6,30},{7,31},{8,16},{9,... | collective-permute-start | bytes 208904 | tf_op jit(solution)/shard_map/ppermute | solution.py:448
  20.0 0.6 collective-permute-start.4
  20.7 1.7 %collective-permute-start.10 = (bf16[4,272,128]{2,1,0:T(8,128)(2,1)S(1)}, bf16[4,272,128]{2,1,0:T(8,128)(2,1)S(1)}, u32[]{:S(2)}, u32[]{:S(2)}) collective-permute-start(bf16[4,272,128]{2,1,0:T(8,128)(2,1)S(1)} %pad_maximum_fusion.after_ref.refs_0_.refs_2_), channel_id=1, source_target_pairs={{0,4},{1,5},{2,6},{3,7},{4,0},{5,1},{6,2},{7,3},{8,12},{9,13},{10,... | collective-permute-start | bytes 835592 | tf_op jit(solution)/shard_map/ppermute | solution.py:448
  22.4 1.5 %collective-permute-start.9 = (bf16[4,272,128]{2,1,0:T(8,128)(2,1)S(1)}, bf16[4,272,128]{2,1,0:T(8,128)(2,1)S(1)}, u32[]{:S(2)}, u32[]{:S(2)}) collective-permute-start(bf16[4,272,128]{2,1,0:T(8,128)(2,1)S(1)} %pad_maximum_fusion.after_ref.refs_0_.refs_2_), channel_id=1, source_target_pairs={{0,2},{1,3},{2,0},{3,1},{4,6},{5,7},{6,4},{7,5},{8,10},{9,11},{10,... | collective-permute-start | bytes 835592 | tf_op jit(solution)/shard_map/ppermute | solution.py:448
  23.8 5.6 %shard_map.93 = (bf16[128,1024]{1,0:T(8,128)(2,1)S(1)}, bf16[128,1024]{1,0:T(8,128)(2,1)S(1)}) custom-call(bf16[16,2,1024,128]{3,2,1,0:T(8,128)(2,1)} %bitcast.34, bf16[8,128]{1,0:T(8,128)(2,1)S(1)} %bitcast.25, bf16[4,272,128]{2,1,0:T(8,128)(2,1)S(1)} %pad_maximum_fusion.after_ref.refs_0_.refs_2_, s32[1]{0:T(128)} %bitcast.me_ref), custom_call_target="tpu_custom_call" | custom-call | flops 4294967296 | bytes 8669188 | tf_op jit(solution)/shard_map/pallas_call | solution.py:438
  29.6 0.6 collective-permute-start.11
  30.2 0.5 collective-permute-start.8
  30.7 1.0 %collective-permute-done.7.peer_even_ref = bf16[128,1024]{1,0:T(8,128)(2,1)S(1)} collective-permute-done((bf16[128,1024]{1,0:T(8,128)(2,1)S(1)}, bf16[128,1024]{1,0:T(8,128)(2,1)S(1)}, u32[]{:S(2)}, u32[]{:S(2)}) %collective-permute-start.7) | collective-permute-done | bytes 262176 | tf_op jit(solution)/shard_map/ppermute | solution.py:448
  31.7 0.4 collective-permute-start.14
  32.1 4.4 %shard_map.94 = (f32[512,1024]{1,0:T(8,128)S(1)}, bf16[16,512,128]{2,1,0:T(8,128)(2,1)S(1)}, f32[16,512,128]{2,1,0:T(8,128)S(1)}, bf16[2048,256]{1,0:T(8,128)(2,...) custom-call(bf16[128,1024]{1,0:T(8,128)(2,1)S(1)} %get-tuple-element.47.even_ref, ...), custom_call_target="tpu_custom_call" | custom-call | tf_op jit(solution)/shard_map/pallas_call | solution.py:438
  36.6 1.7 %collective-permute-start.12 = (bf16[4,272,128]{2,1,0:T(8,128)(2,1)S(1)}, bf16[4,272,128]{2,1,0:T(8,128)(2,1)S(1)}, u32[]{:S(2)}, u32[]{:S(2)}) collective-permute-start(bf16[4,272,128]{2,1,0:T(8,128)(2,1)S(1)} %collective-permute-done.9.refs_0_.refs_4_), channel_id=1, source_target_pairs={{0,4},{1,5},{2,6},{3,7},{4,0},{5,1},{6,2},{7,3},{8,12},{9,13},{10,... | collective-permute-start | bytes 835592 | tf_op jit(solution)/shard_map/ppermute | solution.py:448
  38.3 1.5 %collective-permute-start.13 = (bf16[4,272,128]{2,1,0:T(8,128)(2,1)S(1)}, bf16[4,272,128]{2,1,0:T(8,128)(2,1)S(1)}, u32[]{:S(2)}, u32[]{:S(2)}) collective-permute-start(bf16[4,272,128]{2,1,0:T(8,128)(2,1)S(1)} %collective-permute-done.11.refs_1_.refs_7_), channel_id=1, source_target_pairs={{0,2},{1,3},{2,0},{3,1},{4,6},{5,7},{6,4},{7,5},{8,10},{9,11},{10,... | collective-permute-start | bytes 835592 | tf_op jit(solution)/shard_map/ppermute | solution.py:448
  39.8 2.5 %shard_map.95.before_ref = f32[16,512,128]{2,1,0:T(8,128)S(1)} custom-call(bf16[16,512,128]{2,1,0:T(8,128)(2,1)S(1)} %get-tuple-element.65.lhs_ref, f32[512,1024]{1,0:T(8,128)S(1)} %get-tuple-element.66.bias_ref, f32[16,512,128]{2,1,0:T(8,128)S(1)} %get-tuple-element.70.before_ref, bf16[4,272,128]{2,1,0:T(8,128)(2,1)S(1)} %collective-permute-done.9.refs_0_.refs_4_, ...), custom_call_target="tpu_custom_call" | custom-call | flops 4294967296 | bytes 8945664 | tf_op jit(solution)/shard_map/pallas_call | solution.py:438
  42.3 2.5 %shard_map.96.sums_ref = f32[16,512,128]{2,1,0:T(8,128)S(1)} custom-call(bf16[16,512,128]{2,1,0:T(8,128)(2,1)S(1)} %get-tuple-element.65.lhs_ref, f32[512,1024]{1,0:T(8,128)S(1)} %get-tuple-element.66.bias_ref, f32[16,512,128]{2,1,0:T(8,128)S(1)} %shard_map.95.before_ref, bf16[4,272,128]{2,1,0:T(8,128)(2,1)S(1)} %collective-permute-done.10.refs_0_.refs_6_, ...), custom_call_target="tpu_custom_call" | custom-call | flops 4294967296 | bytes 8945664 | tf_op jit(solution)/shard_map/pallas_call | solution.py:438
  44.7 0.6 collective-permute-done.12.refs_0_
  45.3 1.2 %collective-permute-done.13.refs_1_ = bf16[4,272,128]{2,1,0:T(8,128)(2,1)S(1)} collective-permute-done((bf16[4,272,128]{2,1,0:T(8,128)(2,1)S(1)}, bf16[4,272,128]{2,1,0:T(8,128)(2,1)S(1)}, u32[]{:S(2)}, u32[]{:S(2)}) %collective-permute-start.13) | collective-permute-done | bytes 278560 | tf_op jit(solution)/shard_map/ppermute | solution.py:448
  46.5 26.8 %shard_map.97 = (bf16[256,128]{1,0:T(8,128)(2,1)S(1)}, bf16[256,128]{1,0:T(8,128)(2,1)S(1)}) custom-call(bf16[16,512,128]{2,1,0:T(8,128)(2,1)S(1)} %get-tuple-element.65.lhs_ref, f32[512,1024]{1,0:T(8,128)S(1)} %get-tuple-element.66.bias_ref, f32[16,512,128]{2,1,0:T(8,128)S(1)} %shard_map.96.sums_ref, bf16[2048,256]{1,0:T(8,128)(2,1)S(1)} %get-tuple-element.73.wv_ref, ...), custom_call_target="tpu_custom_call" | custom-call | flops 2147483648 | bytes 11927552 | tf_op jit(solution)/shard_map/pallas_call | solution.py:438
  73.3 0.1 collective-permute-start.15
  73.4 1.2 %collective-permute-done.15.theirs_ref = bf16[256,128]{1,0:T(8,128)(2,1)S(1)} collective-permute-done((bf16[256,128]{1,0:T(8,128)(2,1)S(1)}, bf16[256,128]{1,0:T(8,128)(2,1)S(1)}, u32[]{:S(2)}, u32[]{:S(2)}) %collective-permute-start.15) | collective-permute-done | bytes 65568 | tf_op jit(solution)/shard_map/ppermute | solution.py:448
  74.6 2.3 %shard_map.98 = bf16[32,2048]{1,0:T(8,128)(2,1)} custom-call(s32[1]{0:T(128)} %bitcast.me_ref, bf16[512,128]{1,0:T(8,128)(2,1)S(1)} %get-tuple-element.42.line_ref, f32[512,128]{1,0:T(8,128)S(1)} %get-tuple-element.63.kept_ref, bf16[128,768]{1,0:T(8,128)(2,1)S(1)} %get-tuple-element.64.w_ref, bf16[256,128]{1,0:T(8,128)(2,1)S(1)} %get-tuple-element.77.mine_ref, ...), custom_call_target="tpu_custom_call" | custom-call | bytes 720900 | tf_op jit(solution)/shard_map/pallas_call | solution.py:438
  (30 shorter events, 0.2 us)
Async XLA Ops:
  0.7 0.9 %copy-start = (bf16[32,2048]{1,0:T(8,128)(2,1)S(1)}, bf16[32,2048]{1,0:T(8,128)(2,1)}, u32[]{:S(2)}) copy-start(bf16[32,2048]{1,0:T(8,128)(2,1)} %m_ref.1) | copy-start | bytes 393220
  2.8 1.4 %collective-permute-start = (bf16[2,144,128]{2,1,0:T(8,128)(2,1)S(1)}, bf16[2,144,128]{2,1,0:T(8,128)(2,1)S(1)}, u32[]{:S(2)}, u32[]{:S(2)}) collective-permute-start(bf16[2,144,128]{2,1,0:T(8,128)(2,1)S(1)} %get-tuple-element.44), channel_id=1, source_target_pairs={{0,1},{1,0},{2,3},{3,2},{4,5},{5,4},{6,7},{7,6},{8,9},{9,8},{10,11... | collective-permute-start | bytes 221192 | tf_op jit(solution)/shard_map/ppermute | solution.py:448
  4.3 11.8 %collective-permute-start.3 = (bf16[272,128]{1,0:T(8,128)(2,1)S(1)}, bf16[272,128]{1,0:T(8,128)(2,1)S(1)}, u32[]{:S(2)}, u32[]{:S(2)}) collective-permute-start(bf16[272,128]{1,0:T(8,128)(2,1)S(1)} %pad_maximum_fusion.2.after_ref), channel_id=1, source_target_pairs={{0,24},{1,25},{2,26},{3,27},{4,28},{5,29},{6,30},{7,31},{8,16},{9,... | collective-permute-start | bytes 208904 | tf_op jit(solution)/shard_map/ppermute | solution.py:448
  9.3 6.8 %collective-permute-start.2 = (bf16[272,128]{1,0:T(8,128)(2,1)S(1)}, bf16[272,128]{1,0:T(8,128)(2,1)S(1)}, u32[]{:S(2)}, u32[]{:S(2)}) collective-permute-start(bf16[272,128]{1,0:T(8,128)(2,1)S(1)} %pad_maximum_fusion.2.after_ref), channel_id=1, source_target_pairs={{0,16},{1,17},{2,18},{3,19},{4,20},{5,21},{6,22},{7,23},{8,24},{9,... | collective-permute-start | bytes 208904 | tf_op jit(solution)/shard_map/ppermute | solution.py:448
  9.3 6.8 %collective-permute-start.1 = (bf16[272,128]{1,0:T(8,128)(2,1)S(1)}, bf16[272,128]{1,0:T(8,128)(2,1)S(1)}, u32[]{:S(2)}, u32[]{:S(2)}) collective-permute-start(bf16[272,128]{1,0:T(8,128)(2,1)S(1)} %pad_maximum_fusion.2.after_ref), channel_id=1, source_target_pairs={{0,8},{1,9},{2,10},{3,11},{4,12},{5,13},{6,14},{7,15},{8,0},{9,1},... | collective-permute-start | bytes 208904 | tf_op jit(solution)/shard_map/ppermute | solution.py:448
  9.9 0.7 copy-start.5
  10.6 13.2 %copy-start.6 = (bf16[128,8]{0,1:T(8,128)(2,1)S(1)}, bf16[128,8]{0,1:T(8,128)(2,1)}, u32[]{:S(2)}) copy-start(bf16[128,8]{0,1:T(8,128)(2,1)} %param.13) | copy-start | bytes 6148
  16.2 15.9 %copy-start.1 = (bf16[64,256]{1,0:T(8,128)(2,1)S(1)}, bf16[64,256]{1,0:T(8,128)(2,1)}, u32[]{:S(2)}) copy-start(bf16[64,256]{1,0:T(8,128)(2,1)} %w_ref.1) | copy-start | bytes 98308
  16.2 15.9 %copy-start.2 = (bf16[64,144]{1,0:T(8,128)(2,1)S(1)}, bf16[64,144]{1,0:T(8,128)(2,1)}, u32[]{:S(2)}) copy-start(bf16[64,144]{1,0:T(8,128)(2,1)} %column_ref.1) | copy-start | bytes 55300
  16.2 15.9 %copy-start.3 = (bf16[64,64]{1,0:T(8,128)(2,1)S(1)}, bf16[64,64]{1,0:T(8,128)(2,1)}, u32[]{:S(2)}) copy-start(bf16[64,64]{1,0:T(8,128)(2,1)} %exit_ref.1) | copy-start | bytes 24580
  16.2 15.9 %copy-start.4 = (bf16[64,64]{1,0:T(8,128)(2,1)S(1)}, bf16[64,64]{1,0:T(8,128)(2,1)}, u32[]{:S(2)}) copy-start(bf16[64,64]{1,0:T(8,128)(2,1)} %column_exit_ref.1) | copy-start | bytes 24580
  16.2 13.3 %collective-permute-start.6 = (bf16[272,128]{1,0:T(8,128)(2,1)S(1)}, bf16[272,128]{1,0:T(8,128)(2,1)S(1)}, u32[]{:S(2)}, u32[]{:S(2)}) collective-permute-start(bf16[272,128]{1,0:T(8,128)(2,1)S(1)} %pad_maximum_fusion.3), channel_id=1, source_target_pairs={{0,24},{1,25},{2,26},{3,27},{4,28},{5,29},{6,30},{7,31},{8,16},{9,... | collective-permute-start | bytes 208904 | tf_op jit(solution)/shard_map/ppermute | solution.py:448
  20.0 9.5 %collective-permute-start.5 = (bf16[272,128]{1,0:T(8,128)(2,1)S(1)}, bf16[272,128]{1,0:T(8,128)(2,1)S(1)}, u32[]{:S(2)}, u32[]{:S(2)}) collective-permute-start(bf16[272,128]{1,0:T(8,128)(2,1)S(1)} %pad_maximum_fusion.3), channel_id=1, source_target_pairs={{0,16},{1,17},{2,18},{3,19},{4,20},{5,21},{6,22},{7,23},{8,24},{9,... | collective-permute-start | bytes 208904 | tf_op jit(solution)/shard_map/ppermute | solution.py:448
  20.0 9.5 %collective-permute-start.4 = (bf16[272,128]{1,0:T(8,128)(2,1)S(1)}, bf16[272,128]{1,0:T(8,128)(2,1)S(1)}, u32[]{:S(2)}, u32[]{:S(2)}) collective-permute-start(bf16[272,128]{1,0:T(8,128)(2,1)S(1)} %pad_maximum_fusion.3), channel_id=1, source_target_pairs={{0,8},{1,9},{2,10},{3,11},{4,12},{5,13},{6,14},{7,15},{8,0},{9,1},... | collective-permute-start | bytes 208904 | tf_op jit(solution)/shard_map/ppermute | solution.py:448
  20.7 15.8 %collective-permute-start.10 = (bf16[4,272,128]{2,1,0:T(8,128)(2,1)S(1)}, bf16[4,272,128]{2,1,0:T(8,128)(2,1)S(1)}, u32[]{:S(2)}, u32[]{:S(2)}) collective-permute-start(bf16[4,272,128]{2,1,0:T(8,128)(2,1)S(1)} %pad_maximum_fusion.after_ref.refs_0_.refs_2_), channel_id=1, source_target_pairs={{0,4},{1,5},{2,6},{3,7},{4,0},{5,1},{6,2},{7,3},{8,12},{9,13},{10,... | collective-permute-start | bytes 835592 | tf_op jit(solution)/shard_map/ppermute | solution.py:448
  22.4 14.2 %collective-permute-start.9 = (bf16[4,272,128]{2,1,0:T(8,128)(2,1)S(1)}, bf16[4,272,128]{2,1,0:T(8,128)(2,1)S(1)}, u32[]{:S(2)}, u32[]{:S(2)}) collective-permute-start(bf16[4,272,128]{2,1,0:T(8,128)(2,1)S(1)} %pad_maximum_fusion.after_ref.refs_0_.refs_2_), channel_id=1, source_target_pairs={{0,2},{1,3},{2,0},{3,1},{4,6},{5,7},{6,4},{7,5},{8,10},{9,11},{10,... | collective-permute-start | bytes 835592 | tf_op jit(solution)/shard_map/ppermute | solution.py:448
  29.6 7.0 %collective-permute-start.11 = (bf16[4,272,128]{2,1,0:T(8,128)(2,1)S(1)}, bf16[4,272,128]{2,1,0:T(8,128)(2,1)S(1)}, u32[]{:S(2)}, u32[]{:S(2)}) collective-permute-start(bf16[4,272,128]{2,1,0:T(8,128)(2,1)S(1)} %pad_maximum_fusion.1.refs_1_.refs_3_), channel_id=1, source_target_pairs={{0,4},{1,5},{2,6},{3,7},{4,0},{5,1},{6,2},{7,3},{8,12},{9,13},{10,... | collective-permute-start | bytes 835592 | tf_op jit(solution)/shard_map/ppermute | solution.py:448
  30.1 1.5 %collective-permute-start.7 = (bf16[128,1024]{1,0:T(8,128)(2,1)S(1)}, bf16[128,1024]{1,0:T(8,128)(2,1)S(1)}, u32[]{:S(2)}, u32[]{:S(2)}) collective-permute-start(bf16[128,1024]{1,0:T(8,128)(2,1)S(1)} %get-tuple-element.57), channel_id=1, source_target_pairs={{0,1},{1,0},{2,3},{3,2},{4,5},{5,4},{6,7},{7,6},{8,9},{9,8},{10,11... | collective-permute-start | bytes 786440 | tf_op jit(solution)/shard_map/ppermute | solution.py:448
  30.2 1.9 %collective-permute-start.8 = (bf16[128,1024]{1,0:T(8,128)(2,1)S(1)}, bf16[128,1024]{1,0:T(8,128)(2,1)S(1)}, u32[]{:S(2)}, u32[]{:S(2)}) collective-permute-start(bf16[128,1024]{1,0:T(8,128)(2,1)S(1)} %get-tuple-element.58), channel_id=1, source_target_pairs={{0,1},{1,0},{2,3},{3,2},{4,5},{5,4},{6,7},{7,6},{8,9},{9,8},{10,11... | collective-permute-start | bytes 786440 | tf_op jit(solution)/shard_map/ppermute | solution.py:448
  31.7 10.6 %collective-permute-start.14 = (bf16[4,272,128]{2,1,0:T(8,128)(2,1)S(1)}, bf16[4,272,128]{2,1,0:T(8,128)(2,1)S(1)}, u32[]{:S(2)}, u32[]{:S(2)}) collective-permute-start(bf16[4,272,128]{2,1,0:T(8,128)(2,1)S(1)} %pad_maximum_fusion.1.refs_1_.refs_3_), channel_id=1, source_target_pairs={{0,2},{1,3},{2,0},{3,1},{4,6},{5,7},{6,4},{7,5},{8,10},{9,11},{10,... | collective-permute-start | bytes 835592 | tf_op jit(solution)/shard_map/ppermute | solution.py:448
  36.6 8.7 %collective-permute-start.12 = (bf16[4,272,128]{2,1,0:T(8,128)(2,1)S(1)}, bf16[4,272,128]{2,1,0:T(8,128)(2,1)S(1)}, u32[]{:S(2)}, u32[]{:S(2)}) collective-permute-start(bf16[4,272,128]{2,1,0:T(8,128)(2,1)S(1)} %collective-permute-done.9.refs_0_.refs_4_), channel_id=1, source_target_pairs={{0,4},{1,5},{2,6},{3,7},{4,0},{5,1},{6,2},{7,3},{8,12},{9,13},{10,... | collective-permute-start | bytes 835592 | tf_op jit(solution)/shard_map/ppermute | solution.py:448
  38.3 8.2 %collective-permute-start.13 = (bf16[4,272,128]{2,1,0:T(8,128)(2,1)S(1)}, bf16[4,272,128]{2,1,0:T(8,128)(2,1)S(1)}, u32[]{:S(2)}, u32[]{:S(2)}) collective-permute-start(bf16[4,272,128]{2,1,0:T(8,128)(2,1)S(1)} %collective-permute-done.11.refs_1_.refs_7_), channel_id=1, source_target_pairs={{0,2},{1,3},{2,0},{3,1},{4,6},{5,7},{6,4},{7,5},{8,10},{9,11},{10,... | collective-permute-start | bytes 835592 | tf_op jit(solution)/shard_map/ppermute | solution.py:448
  73.3 1.3 %collective-permute-start.15 = (bf16[256,128]{1,0:T(8,128)(2,1)S(1)}, bf16[256,128]{1,0:T(8,128)(2,1)S(1)}, u32[]{:S(2)}, u32[]{:S(2)}) collective-permute-start(bf16[256,128]{1,0:T(8,128)(2,1)S(1)} %get-tuple-element.78), channel_id=1, source_target_pairs={{0,1},{1,0},{2,3},{3,2},{4,5},{5,4},{6,7},{7,6},{8,9},{9,8},{10,11... | collective-permute-start | bytes 196616 | tf_op jit(solution)/shard_map/ppermute | solution.py:448
